TPU v7x, 32 devices: a whole 2x2x4 slice. The times are simulated.
32 devices in a mesh: feat: 2 (over x), layer: 4 (over z), tok: 4 (over y, core).
Axes of the slice: x: 2, y: 2, z: 4, core: 2. Of those that a mesh axis runs over, the one named last changes fastest.
Arguments:
- captured: bfloat16 [4, 512, 2304], P('layer', 'tok', 'feat'), may hold values from -6 to 6
- target: bfloat16 [4, 512, 2304], P('layer', 'feat', 'tok'), may hold values from -6 to 6
- enc_weight: bfloat16 [4, 2304, 2048], P('layer', 'tok', 'feat'), may hold values from -0.125 to 0.125
- enc_bias: float32 [4, 2048], P('layer', 'feat'), may hold values from -3 to 3
- dec_weight: bfloat16 [4, 4, 2048, 2304], P('layer', None, 'feat', 'tok'), may hold values from -0.09375 to 0.09375
- dec_bias: float32 [4, 2304], P('layer', 'tok'), may hold values from -3 to 3
Outputs:
- enc_weight_grad: bfloat16 [4, 2304, 2048], P('layer', 'tok', 'feat')
- enc_bias_grad: float32 [4, 2048], P('layer', 'feat')
- dec_weight_grad: bfloat16 [4, 4, 2048, 2304], P('layer', None, 'feat', 'tok')
- dec_bias_grad: float32 [4, 2304], P('layer', 'tok')
All inputs are finite; a program needn't handle non-finite values.
Results may differ from a plain program's by a relative error of at most 0.008.
Values may be sent and summed in bfloat16 or wider, within the bound.
A program may use at most 64 MiB of HBM per device.

v0:
```python
import math

import jax
import jax.numpy as jnp
from jax import lax
from jax.sharding import PartitionSpec as P


def contract_rows(left, right):
    return lax.dot_general(
        left, right, (((0,), (0,)), ((), ())), preferred_element_type=jnp.float32
    )


def on_device(captured, target, enc_weight, enc_bias, dec_weight, dec_bias):
    layer = lax.axis_index("layer")
    nlayer = dec_weight.shape[1]
    feat_cols = enc_weight.shape[2]
    width_part = enc_weight.shape[1]
    total_tokens = target.shape[1] * lax.axis_size("feat")
    scale = 1.0 / math.sqrt(total_tokens)
    encoder = enc_weight[0]
    rows = lax.all_gather(captured[0], "feat", axis=1, tiled=True)
    moved = lax.all_to_all(rows, "tok", split_axis=1, concat_axis=0, tiled=True)
    block = moved
    pre = (
        lax.psum_scatter(
            jnp.dot(block, encoder, preferred_element_type=jnp.float32),
            "tok",
            scatter_dimension=0,
            tiled=True,
        )
        + enc_bias
    )
    act = jnp.maximum(pre, 0.0).astype(jnp.bfloat16)
    act_all = lax.all_gather(act, "tok", axis=0, tiled=True)
    all_tokens = act_all.shape[0]

    def decode_step(write, partial_value):
        weight = lax.dynamic_index_in_dim(dec_weight[0], write, 0, keepdims=False)
        output = jnp.dot(act_all, weight, preferred_element_type=jnp.float32)
        return lax.dynamic_update_index_in_dim(partial_value, output, write, 0)

    partial_value = jnp.zeros((nlayer, all_tokens, width_part), jnp.float32)
    partial_value = lax.fori_loop(layer, nlayer, decode_step, partial_value)
    shared = lax.psum_scatter(partial_value, "feat", scatter_dimension=1, tiled=True)
    recon = lax.psum_scatter(shared, "layer", scatter_dimension=0, tiled=True)
    err = recon + dec_bias[:, None, :] - target.astype(jnp.float32)
    scaled = err * scale
    dec_bias_grad = lax.psum(jnp.sum(scaled, axis=1), "feat")
    grad_out = scaled.astype(jnp.bfloat16)
    spread = lax.all_gather(grad_out, "layer", axis=0, tiled=True)
    grad_all = lax.all_gather(spread, "feat", axis=1, tiled=True)

    def back_step(write, carry):
        dec_grads, grad_act = carry
        weight = lax.dynamic_index_in_dim(dec_weight[0], write, 0, keepdims=False)
        upstream = lax.dynamic_index_in_dim(grad_all, write, 0, keepdims=False)
        block = contract_rows(act_all, upstream).astype(jnp.bfloat16)
        dec_grads = lax.dynamic_update_index_in_dim(dec_grads, block, write, 0)
        grad_act = grad_act + lax.dot_general(
            upstream, weight, (((1,), (1,)), ((), ())), preferred_element_type=jnp.float32
        )
        return (dec_grads, grad_act)

    dec_start = jnp.zeros((nlayer, feat_cols, width_part), jnp.bfloat16)
    act_start = jnp.zeros((all_tokens, feat_cols), jnp.float32)
    dec_grads, grad_act = lax.fori_loop(layer, nlayer, back_step, (dec_start, act_start))
    grad_mine = lax.psum_scatter(grad_act, "tok", scatter_dimension=0, tiled=True)
    grad_pre = jnp.where(pre > 0, grad_mine, 0.0).astype(jnp.bfloat16)
    grad_every = lax.all_gather(grad_pre, "tok", axis=0, tiled=True)
    enc_bias_grad = jnp.sum(grad_every.astype(jnp.float32), axis=0)
    enc_grad = contract_rows(moved, grad_every)
    return (
        enc_grad.astype(jnp.bfloat16)[None],
        enc_bias_grad[None],
        dec_grads[None],
        dec_bias_grad,
    )


def solution(mesh):
    in_specs = (
        P("layer", "tok", "feat"),
        P("layer", "feat", "tok"),
        P("layer", "tok", "feat"),
        P("layer", "feat"),
        P("layer", None, "feat", "tok"),
        P("layer", "tok"),
    )
    out_specs = (
        P("layer", "tok", "feat"),
        P("layer", "feat"),
        P("layer", None, "feat", "tok"),
        P("layer", "tok"),
    )
    return jax.shard_map(
        on_device, mesh=mesh, in_specs=in_specs, out_specs=out_specs, check_vma=False
    )
```

profile of v0, /device:TPU:0, one launch (start us, length us, event | category | flops | bytes accessed | tf_op | source)
XLA Modules:
  0.0 362.8 jit_solution(17983596374788221743)
XLA Ops:
  8.5 10.6 %all-gather = bf16[1,128,2304]{1,2,0:T(8,128)(2,1)S(1)} all-gather(bf16[1,128,1152]{1,2,0:T(8,128)(2,1)S(1)} %copy.16), channel_id=2, replica_groups=mesh['feat'=2,'layer'=4,'tok'=4] {'feat'}, dimensions={2}, use_global_device_ids=true | all-gather | bytes 884736 | tf_op jit(solution)/shard_map/all_gather | solution.py:23
  19.1 12.4 %all_to_all.19 = bf16[128,4,576]{0,2,1:T(8,128)(2,1)S(1)} all-to-all(bf16[128,4,576]{0,2,1:T(8,128)(2,1)S(1)} %bitcast.69), channel_id=1, replica_groups=mesh['feat'=2,'layer'=4,'tok'=4] {'tok'}, dimensions={1} | all-to-all | bytes 1179648 | tf_op jit(solution)/shard_map/all_to_all | solution.py:24
  34.7 31.8 %reduce-scatter.5.cloned.1.call-done = f32[128,1024]{1,0:T(8,128)} async-done(((f32[512,1024]{1,0:T(8,128)}), f32[128,1024]{1,0:T(8,128)}) %reduce-scatter.5.cloned.1.call-update) | async-done | bytes 524304 | tf_op jit(solution)/shard_map/reduce_scatter | solution.py:27
  68.4 17.1 %all-gather.6.cloned.1.call-done = bf16[512,1024]{1,0:T(8,128)(2,1)} async-done(((bf16[128,1024]{1,0:T(8,128)(2,1)}), bf16[512,1024]{1,0:T(8,128)(2,1)}) %all-gather.6.cloned.1.call-update) | async-done | bytes 1048592 | tf_op jit(solution)/shard_map/all_gather | solution.py:36
  85.5 2.8 broadcast_in_dim.31
  88.3 12.4 %while.22 = (s32[]{:T(128)}, f32[4,512,576]{1,2,0:T(8,128)}, bf16[1,4,1024,576]{2,3,1,0:T(8,128)(2,1)}, bf16[512,1024]{1,0:T(8,128)(2,1)S(1)}, s32[]{:T(128)}, /*index=5*/s32[]{:T(128)}, s32[]{:T(128)}) while((s32[]{:T(128)}, f32[4,512,576]{1,2,0:T(8,128)}, bf16[1,4,1024,576]{2,3,1,0:T(8,128)(2,1)}, bf16[512,1024]{1,0:T(8,128)(2,1)S(1)}, ...), condition=%wide.region_2.3_spmd, body=%wide.region_1.2_spmd.sunk | while | flops 603979776 | bytes 3409015 | solution.py:45
  88.3 3.1 fusion.38
  91.4 3.1 fusion.38
  94.5 3.1 fusion.38
  97.6 3.1 fusion.38
  100.8 57.3 %reduce-scatter.7.cloned.1.call-done = f32[4,256,576]{1,2,0:T(8,128)} async-done(((f32[4,512,576]{1,2,0:T(8,128)}), f32[4,256,576]{1,2,0:T(8,128)}) %reduce-scatter.7.cloned.1.call-update) | async-done | bytes 2359312 | tf_op jit(solution)/shard_map/reduce_scatter | solution.py:46
  158.2 50.1 %reduce-scatter.9.cloned.1.call-done = f32[1,256,576]{1,2,0:T(8,128)} async-done(((f32[4,256,576]{1,2,0:T(8,128)}), f32[1,256,576]{1,2,0:T(8,128)}) %reduce-scatter.9.cloned.1.call-update) | async-done | bytes 589840 | tf_op jit(solution)/shard_map/reduce_scatter | solution.py:47
  210.3 30.1 %all-gather.8.cloned.1.call-done = bf16[4,256,576]{1,2,0:T(8,128)(2,1)} async-done(((bf16[1,256,576]{1,2,0:T(8,128)(2,1)}), bf16[4,256,576]{1,2,0:T(8,128)(2,1)}) %all-gather.8.cloned.1.call-update) | async-done | bytes 1179664 | tf_op jit(solution)/shard_map/all_gather | solution.py:52
  240.5 36.5 %all-gather.10.cloned.1.call-done = bf16[4,512,576]{1,2,0:T(8,128)(2,1)} async-done(((bf16[4,256,576]{1,2,0:T(8,128)(2,1)}), bf16[4,512,576]{1,2,0:T(8,128)(2,1)}) %all-gather.10.cloned.1.call-update) | async-done | bytes 2359312 | tf_op jit(solution)/shard_map/all_gather | solution.py:53
  277.2 2.8 broadcast_in_dim.29
  280.0 21.9 %while.23 = (s32[]{:T(128)}, bf16[4,1024,576]{1,2,0:T(8,128)(2,1)}, f32[512,1024]{1,0:T(8,128)S(1)}, bf16[4,512,576]{1,2,0:T(8,128)(2,1)}, bf16[512,1024]{1,0:T(...) while((s32[]{:T(128)}, bf16[4,1024,576]{1,2,0:T(8,128)(2,1)}, ...), condition=%wide.region_6.7_spmd, body=%wide.region_5.6_spmd.sunk | while | flops 1209073664 | bytes 12978339 | solution.py:68
  282.6 2.9 fusion.43
  288.1 2.9 fusion.43
  293.5 2.9 fusion.43
  299.0 2.9 fusion.43
  303.3 28.8 %reduce-scatter.11.cloned.1.call-done = f32[128,1024]{1,0:T(8,128)} async-done(((f32[512,1024]{1,0:T(8,128)}), f32[128,1024]{1,0:T(8,128)}) %reduce-scatter.11.cloned.1.call-update) | async-done | bytes 524304 | tf_op jit(solution)/shard_map/reduce_scatter | solution.py:69
  334.1 5.5 %psum.7 = f32[1,576]{1,0:T(1,128)} all-reduce(f32[1,576]{1,0:T(1,128)S(1)} %reduce_sum.22), channel_id=1, replica_groups=mesh['feat'=2,'layer'=4,'tok'=4] {'feat'}, use_global_device_ids=true, to_apply=%region_10.11 | all-reduce | flops 576 | bytes 4608 | tf_op jit(solution)/shard_map/psum | solution.py:50
  339.6 11.3 %all-gather.12.cloned.1.call-done = bf16[512,1024]{1,0:T(8,128)(2,1)} async-done(((bf16[128,1024]{1,0:T(8,128)(2,1)}), bf16[512,1024]{1,0:T(8,128)(2,1)}) %all-gather.12.cloned.1.call-update) | async-done | bytes 1048592 | tf_op jit(solution)/shard_map/all_gather | solution.py:71
  353.0 3.0 fusion.14
  (53 shorter events, 24.5 us)
Async XLA Ops:
  7.2 25.1 %copy-start = (bf16[1,576,1024]{2,1,0:T(8,128)(2,1)S(1)}, bf16[1,576,1024]{2,1,0:T(8,128)(2,1)}, u32[]{:S(2)}) copy-start(bf16[1,576,1024]{2,1,0:T(8,128)(2,1)} %param.12) | copy-start | bytes 3538948
  7.2 59.3 %reduce-scatter.5.cloned.1.call-start = ((), (), s32[]{:S(2)}) async-start(), calls=%async_computation.5 | async-start | bytes 2621440 | tf_op jit(solution)/shard_map/reduce_scatter | solution.py:27
  31.5 0.8 copy-start.2
  32.3 34.2 %copy-start.5 = (f32[1,1024]{1,0:T(1,128)S(1)}, f32[1,1024]{1,0:T(1,128)}, u32[]{:S(2)}) copy-start(f32[1,1024]{1,0:T(1,128)} %param.13) | copy-start | bytes 12292
  34.6 50.9 %all-gather.6.cloned.1.call-start = ((), (), s32[]{:S(2)}) async-start(), calls=%async_computation.6 | async-start | bytes 1310720 | tf_op jit(solution)/shard_map/all_gather | solution.py:36
  68.3 89.7 %reduce-scatter.7.cloned.1.call-start = ((), (), s32[]{:S(2)}) async-start(), calls=%async_computation.7 | async-start | bytes 7077888 | tf_op jit(solution)/shard_map/reduce_scatter | solution.py:46
  85.5 2.8 copy-start.7
  100.7 57.5 %copy-start.6 = (f32[1,576]{1,0:T(1,128)S(1)}, f32[1,576]{1,0:T(1,128)}, u32[]{:S(2)}) copy-start(f32[1,576]{1,0:T(1,128)} %param.15) | copy-start | bytes 6916
  100.7 107.6 %copy-start.4 = (bf16[1,256,576]{1,2,0:T(8,128)(2,1)S(1)}, bf16[1,256,576]{1,2,0:T(8,128)(2,1)}, u32[]{:S(2)}) copy-start(bf16[1,256,576]{1,2,0:T(8,128)(2,1)} %param.11) | copy-start | bytes 884740
  100.7 107.6 %reduce-scatter.9.cloned.1.call-start = ((), (), s32[]{:S(2)}) async-start(), calls=%async_computation.8 | async-start | bytes 2949120 | tf_op jit(solution)/shard_map/reduce_scatter | solution.py:47
  158.1 82.3 %all-gather.8.cloned.1.call-start = ((), (), s32[]{:S(2)}) async-start(), calls=%async_computation.9 | async-start | bytes 1474560 | tf_op jit(solution)/shard_map/all_gather | solution.py:52
  210.3 66.7 %all-gather.10.cloned.1.call-start = ((), (), s32[]{:S(2)}) async-start(), calls=%async_computation.10 | async-start | bytes 3538944 | tf_op jit(solution)/shard_map/all_gather | solution.py:53
  240.4 91.6 %reduce-scatter.11.cloned.1.call-start = ((), (), s32[]{:S(2)}) async-start(), calls=%async_computation.11 | async-start | bytes 2621440 | tf_op jit(solution)/shard_map/reduce_scatter | solution.py:69
  280.0 2.6 copy-start.8
  285.5 2.6 copy-start.8
  291.0 2.6 copy-start.8
  296.4 2.6 copy-start.8
  301.9 1.3 copy-start.1
  303.3 49.7 %copy-start.3 = (bf16[128,4,576]{0,2,1:T(8,128)(2,1)S(1)}, bf16[128,4,576]{0,2,1:T(8,128)(2,1)}, u32[]{:S(2)}) copy-start(bf16[128,4,576]{0,2,1:T(8,128)(2,1)} %copy-done.2) | copy-start | bytes 1769476
  303.3 47.7 %all-gather.12.cloned.1.call-start = ((), (), s32[]{:S(2)}) async-start(), calls=%async_computation.12 | async-start | bytes 1310720 | tf_op jit(solution)/shard_map/all_gather | solution.py:71
Sparse Core Ops, SparseCore 0:
  34.8 31.7 reduce-scatter.4
  68.7 16.7 all-gather.5
  100.8 57.2 reduce-scatter.6
  160.2 48.0 reduce-scatter.8
  210.4 29.9 all-gather.7
  241.8 35.1 all-gather.9
  303.4 28.6 reduce-scatter.10
  334.2 16.7 all-gather.11
where the time goes:
time: 364 us; the launch traced here: 363 us
  waiting for transfers between devices  263 us (72%)
  matrix products  39.5 us (11%)
  blocking collectives  28.5 us (8%)
  between operations  14.2 us (4%)
  local copies, waits for them, and re-layouts  9.27 us (3%)
  other arithmetic  7.76 us (2%)
    reduce_scatter x1, waiting for transfers between devices, on_device(): lax.psum_scatter(partial_value, 'feat', scatter_dimension=1, tiled=True)  57.3 us
    reduce_scatter x1, waiting for transfers between devices, on_device(): recon = lax.psum_scatter(shared, 'layer', scatter_dimension=0, tiled=True)  50.1 us
    all_gather x1, waiting for transfers between devices, on_device(): grad_all = lax.all_gather(spread, 'feat', axis=1, tiled=True)  36.5 us
    reduce_scatter x1, waiting for transfers between devices, on_device(): lax.psum_scatter(jnp.dot(block, encoder, preferred_element_type=jnp.float...  31.8 us
    all_gather x1, waiting for transfers between devices, on_device(): spread = lax.all_gather(grad_out, 'layer', axis=0, tiled=True)  30.1 us
    reduce_scatter x1, waiting for transfers between devices, on_device(): lax.psum_scatter(grad_act, 'tok', scatter_dimension=0, tiled=True)  28.8 us
    all_gather x1, waiting for transfers between devices, on_device(): act_all = lax.all_gather(act, 'tok', axis=0, tiled=True)  17.1 us
    dot_general x5, matrix products, contract_rows(): lax.dot_general(left, right, (((0,), (0,)), ((), ())), preferred_element_...  14.5 us
  transfers between devices with their start and end apart: 8, of which 8 were waited for; matrix products, arithmetic and copies ran while one was open for 0% of the time, Pallas kernels for 0%

commit v1 on v0

--- a/solution.py
+++ b/solution.py
@@ -1,8 +1,11 @@
+import functools
 import math
 
 import jax
 import jax.numpy as jnp
 from jax import lax
+from jax.experimental import pallas as pl
+from jax.experimental.pallas import tpu as pltpu
 from jax.sharding import PartitionSpec as P
 
 
@@ -79,6 +82,388 @@
     )
 
 
+BF16 = jnp.bfloat16
+F32 = jnp.float32
+MESH = pl.DeviceIdType.MESH
+VMEM_LIMIT = 52 * 1024 * 1024
+
+
+def fused_kernel(
+    sizes, cap, target, enc_hbm, enc_bias, dec_hbm, dec_bias,
+    enc_grad, enc_bias_grad, dec_grad_hbm, dec_bias_grad,
+    enc, dec, blk, blk_t, pre_a, pre_b, pre_ra, pre_rb, pre_own, pre,
+    act, act_t, x_out, x_in, own, z_out, z_in, bias_out, bias_in, grad,
+    acc, back_a, back_b, back_ra, back_rb, grad_pre, dec_out,
+    load_sem, store_sem, cap_send, cap_recv, pair_send, pair_recv,
+    row_send, row_recv, fwd_send, fwd_recv, lay_send, lay_recv, bias_sem,
+):
+    nf, nl, nt, scale = sizes
+    ny = nt // 2
+    f, l, t = lax.axis_index("feat"), lax.axis_index("layer"), lax.axis_index("tok")
+    y, c = t // 2, t % 2
+    sib = y * 2 + (1 - c)
+    other = 1 - f
+    parts, rows, width = cap.shape
+    half = target.shape[0]
+
+    load_enc = pltpu.make_async_copy(enc_hbm, enc, load_sem.at[0])
+    load_dec = pltpu.make_async_copy(dec_hbm, dec, load_sem.at[1])
+    load_enc.start()
+    load_dec.start()
+
+    barrier = pltpu.get_barrier_semaphore()
+    for df in range(nf):
+        for dt in range(nt):
+            if df or dt:
+                where = {"feat": (f + df) % nf, "tok": (t + dt) % nt}
+                pl.semaphore_signal(barrier, inc=1, device_id=where, device_id_type=MESH)
+
+    @pl.when(l > 0)
+    def _():
+        pl.semaphore_signal(barrier, inc=1, device_id={"layer": l - 1}, device_id_type=MESH)
+
+    @pl.when(l < nl - 1)
+    def _():
+        pl.semaphore_signal(barrier, inc=1, device_id={"layer": l + 1}, device_id_type=MESH)
+
+    layer_peers = jnp.where(l > 0, 1, 0) + jnp.where(l < nl - 1, 1, 0)
+    pl.semaphore_wait(barrier, nf * nt - 1 + layer_peers)
+
+    def remote(source, dest, send, recv, **where):
+        return pltpu.make_async_remote_copy(
+            src_ref=source, dst_ref=dest, send_sem=send, recv_sem=recv,
+            device_id=where, device_id_type=MESH,
+        )
+
+    def token_rows(block):
+        return pl.ds(pl.multiple_of(block * rows, rows), rows)
+
+    def half_rows(which):
+        return pl.ds(pl.multiple_of(which * half, half), half)
+
+    def cap_copy(df, p):
+        return remote(
+            cap.at[p], blk.at[token_rows(t)], cap_send.at[df * parts + p], cap_recv.at[t],
+            feat=(f + df) % nf, tok=f * parts + p,
+        )
+
+    for df in reversed(range(nf)):
+        for p in range(parts):
+            if df:
+                cap_copy(df, p).start()
+            else:
+                @pl.when(t == f * parts + p)
+                def _():
+                    blk[token_rows(t), :] = cap[p]
+
+                @pl.when(t != f * parts + p)
+                def _():
+                    cap_copy(0, p).start()
+
+    acc[...] = jnp.zeros_like(acc)
+
+    def zero_step(write, carry):
+        dec_out[write] = jnp.zeros(dec_out.shape[1:], BF16)
+        pltpu.make_async_copy(dec_out.at[write], dec_grad_hbm.at[write], store_sem.at[write]).start()
+        return carry
+
+    lax.fori_loop(0, l, zero_step, 0)
+    load_enc.wait()
+
+    def encode(block):
+        @pl.when(jnp.logical_or(f != t // parts, block != t))
+        def _():
+            remote(
+                cap.at[0], blk.at[token_rows(block)], cap_send.at[0], cap_recv.at[block],
+                feat=f, tok=sib,
+            ).wait_recv()
+        return jnp.dot(blk[token_rows(block), :], enc[...], preferred_element_type=F32)
+
+    def reduce_rows(base, partial, out_a, out_b, in_a, in_b, kept):
+        order = list(range(1, ny)) + [0]
+        firsts, seconds = {}, {}
+        for dy in order:
+            yb = (y + dy) % ny
+            out_a[dy] = partial(yb * 2 + (1 - c)).astype(out_a.dtype)
+            firsts[dy] = remote(
+                out_a.at[dy], in_a.at[dy], pair_send.at[base + dy], pair_recv.at[base + dy], tok=sib
+            )
+            firsts[dy].start()
+            value = partial(yb * 2 + c)
+            if dy == 0:
+                kept[...] = value
+                continue
+            firsts[dy].wait_recv()
+            out_b[dy] = (value + in_a[dy].astype(F32)).astype(out_b.dtype)
+            seconds[dy] = remote(
+                out_b.at[dy], in_b.at[dy], row_send.at[base + dy], row_recv.at[base + dy],
+                tok=yb * 2 + c,
+            )
+            seconds[dy].start()
+
+        def finish():
+            firsts[0].wait_recv()
+            total = kept[...] + in_a[0].astype(F32)
+            for dy in range(1, ny):
+                seconds[dy].wait_recv()
+                total = total + in_b[dy].astype(F32)
+            for copy in list(firsts.values()) + list(seconds.values()):
+                copy.wait_send()
+            return total
+
+        return finish
+
+    def gather_rows(base, ref):
+        mine = ref.at[token_rows(t)]
+        direct = remote(mine, mine, pair_send.at[base], pair_recv.at[base], tok=sib)
+        across = []
+        for dy in range(1, ny):
+            across.append(remote(
+                mine, mine, row_send.at[base + dy], row_recv.at[base + dy],
+                tok=((y + dy) % ny) * 2 + c,
+            ))
+            across[-1].start()
+        direct.start()
+        forwards = []
+        for dy in range(1, ny):
+            across[dy - 1].wait_recv()
+            block = ref.at[token_rows(((y - dy + ny) % ny) * 2 + c)]
+            forwards.append(remote(
+                block, block, fwd_send.at[base + dy], fwd_recv.at[base + dy], tok=sib
+            ))
+            forwards[-1].start()
+        direct.wait_recv()
+        for copy in forwards:
+            copy.wait_recv()
+        for copy in [direct] + across + forwards:
+            copy.wait_send()
+
+    finish = reduce_rows(0, encode, pre_a, pre_b, pre_ra, pre_rb, pre_own)
+    for b in range(nt):
+        blk_t[:, b * rows:(b + 1) * rows] = blk[b * rows:(b + 1) * rows, :].T
+    pre[...] = finish() + enc_bias[...]
+    act[token_rows(t), :] = jnp.maximum(pre[...], 0.0).astype(BF16)
+    gather_rows(ny, act)
+    load_dec.wait()
+
+    def x_copy(write):
+        return remote(
+            x_out.at[write], x_in.at[write], pair_send.at[4 * ny + write],
+            pair_recv.at[4 * ny + write], feat=other,
+        )
+
+    def z_copy(write):
+        return remote(
+            z_out.at[write], z_in.at[write], lay_send.at[write], lay_recv.at[write], layer=l + 1
+        )
+
+    def z_wait(write):
+        remote(
+            z_out.at[write], z_in.at[write], lay_send.at[write], lay_recv.at[write], feat=other
+        ).wait_recv()
+
+    def decode_other(i, carry):
+        write = nl - 1 - i
+        x_out[write] = jnp.dot(
+            act[half_rows(other), :], dec[write], preferred_element_type=F32
+        ).astype(BF16)
+        x_copy(write).start()
+        return carry
+
+    def decode_own(i, carry):
+        write = nl - 1 - i
+        own[write] = jnp.dot(act[half_rows(f), :], dec[write], preferred_element_type=F32)
+        return carry
+
+    def decode_sum(i, carry):
+        write = nl - 1 - i
+        x_copy(write).wait_recv()
+        own[write] += x_in[write].astype(F32)
+
+        @pl.when(l > 0)
+        def _():
+            z_wait(write)
+            own[write] += z_in[write].astype(F32)
+
+        @pl.when(write > l)
+        def _():
+            z_out[write] = own[write].astype(BF16)
+            z_copy(write).start()
+        return carry
+
+    lax.fori_loop(0, nl - l, decode_other, 0)
+    lax.fori_loop(0, nl - l, decode_own, 0)
+    for b in range(nt):
+        act_t[:, b * rows:(b + 1) * rows] = act[b * rows:(b + 1) * rows, :].T
+    lax.fori_loop(0, nl - l, decode_sum, 0)
+
+    scaled = (own[l] + dec_bias[...] - target[...].astype(F32)) * scale
+    grad[l, half_rows(f), :] = scaled.astype(BF16)
+
+    def down_copy(write):
+        tile = grad.at[write, half_rows(f)]
+        return remote(
+            tile, tile, lay_send.at[nl + write], lay_recv.at[nl + write], layer=l - 1
+        )
+
+    def down_wait(write):
+        tile = grad.at[write, half_rows(f)]
+        remote(
+            tile, tile, lay_send.at[nl + write], lay_recv.at[nl + write], feat=other
+        ).wait_recv()
+
+    def across_copy(write):
+        tile = grad.at[write, half_rows(f)]
+        return remote(
+            tile, tile, pair_send.at[4 * ny + nl + write], pair_recv.at[4 * ny + nl + write],
+            feat=other,
+        )
+
+    def across_wait(write):
+        tile = grad.at[write, half_rows(other)]
+        remote(
+            tile, tile, pair_send.at[4 * ny + nl + write], pair_recv.at[4 * ny + nl + write],
+            feat=other,
+        ).wait_recv()
+
+    def pass_on(write):
+        @pl.when(l > 0)
+        def _():
+            down_copy(write).start()
+        across_copy(write).start()
+
+    pass_on(l)
+    bias_out[...] = jnp.broadcast_to(jnp.sum(scaled, axis=0, keepdims=True), bias_out.shape)
+    bias_copy = remote(bias_out, bias_in, bias_sem.at[0], bias_sem.at[1], feat=other)
+    bias_copy.start()
+
+    def dec_grad_of(write):
+        dec_out[write] = jnp.dot(act_t[...], grad[write], preferred_element_type=F32).astype(BF16)
+        pltpu.make_async_copy(dec_out.at[write], dec_grad_hbm.at[write], store_sem.at[write]).start()
+
+    def back_step(write, carry):
+        @pl.when(write < nl - 1)
+        def _():
+            down_wait(write + 1)
+            pass_on(write + 1)
+        across_wait(write)
+        acc[...] += lax.dot_general(
+            grad[write], dec[write], (((1,), (1,)), ((), ())), preferred_element_type=F32
+        )
+
+        @pl.when(write < nl - 1)
+        def _():
+            dec_grad_of(write)
+        return carry
+
+    lax.fori_loop(l, nl, back_step, 0)
+
+    finish = reduce_rows(
+        2 * ny, lambda block: acc[token_rows(block), :], back_a, back_b, back_ra, back_rb, pre_own
+    )
+    dec_grad_of(nl - 1)
+    grad_pre[token_rows(t), :] = jnp.where(pre[...] > 0, finish(), 0.0).astype(BF16)
+    gather_rows(3 * ny, grad_pre)
+    enc_grad[...] = jnp.dot(blk_t[...], grad_pre[...], preferred_element_type=F32).astype(BF16)
+    enc_bias_grad[...] = jnp.sum(grad_pre[...].astype(F32), axis=0, keepdims=True)
+    bias_copy.wait()
+    dec_bias_grad[...] = bias_out[0:1, :] + bias_in[0:1, :]
+
+    for df in range(nf):
+        for p in range(parts):
+            if df:
+                cap_copy(df, p).wait_send()
+            else:
+                @pl.when(t != f * parts + p)
+                def _():
+                    cap_copy(0, p).wait_send()
+
+    def drain(write, carry):
+        x_copy(write).wait_send()
+        across_copy(write).wait_send()
+
+        @pl.when(write > l)
+        def _():
+            z_copy(write).wait_send()
+
+        @pl.when(l > 0)
+        def _():
+            down_copy(write).wait_send()
+        return carry
+
+    lax.fori_loop(l, nl, drain, 0)
+    for write in range(nl):
+        pltpu.make_async_copy(dec_out.at[write], dec_grad_hbm.at[write], store_sem.at[write]).wait()
+
+
+def on_device_fused(mesh, captured, target, enc_weight, enc_bias, dec_weight, dec_bias):
+    nf, nl, nt = (mesh.shape[name] for name in ("feat", "layer", "tok"))
+    ny = nt // 2
+    width, cols = enc_weight.shape[1:]
+    rows = captured.shape[1]
+    half = target.shape[1]
+    tokens = rows * nt
+    parts = captured.shape[2] // width
+    cap = captured[0].reshape(rows, parts, width).transpose(1, 0, 2)
+    sizes = (nf, nl, nt, 1.0 / math.sqrt(tokens))
+    vm = pl.BlockSpec(memory_space=pltpu.VMEM)
+    hbm = pl.BlockSpec(memory_space=pl.ANY)
+    dma = pltpu.SemaphoreType.DMA
+    block32 = pltpu.VMEM((ny, rows, cols), F32)
+    block16 = pltpu.VMEM((ny, rows, cols), BF16)
+    tile16 = pltpu.VMEM((nl, half, width), BF16)
+    flops = 2 * tokens * width * cols * (2 + 3 * nl)
+    out = pl.pallas_call(
+        functools.partial(fused_kernel, sizes),
+        out_shape=(
+            jax.ShapeDtypeStruct((width, cols), BF16),
+            jax.ShapeDtypeStruct((1, cols), F32),
+            jax.ShapeDtypeStruct((nl, cols, width), BF16),
+            jax.ShapeDtypeStruct((1, width), F32),
+        ),
+        in_specs=[vm, vm, hbm, vm, hbm, vm],
+        out_specs=(vm, vm, hbm, vm),
+        scratch_shapes=[
+            pltpu.VMEM((width, cols), BF16),
+            pltpu.VMEM((nl, cols, width), BF16),
+            pltpu.VMEM((tokens, width), BF16),
+            pltpu.VMEM((width, tokens), BF16),
+            block32, block32, block32, block32,
+            pltpu.VMEM((rows, cols), F32),
+            pltpu.VMEM((rows, cols), F32),
+            pltpu.VMEM((tokens, cols), BF16),
+            pltpu.VMEM((cols, tokens), BF16),
+            tile16, tile16,
+            pltpu.VMEM((nl, half, width), F32),
+            tile16, tile16,
+            pltpu.VMEM((8, width), F32),
+            pltpu.VMEM((8, width), F32),
+            pltpu.VMEM((nl, tokens, width), BF16),
+            pltpu.VMEM((tokens, cols), F32),
+            block16, block16, block16, block16,
+            pltpu.VMEM((tokens, cols), BF16),
+            pltpu.VMEM((nl, cols, width), BF16),
+            dma((2,)), dma((nl,)),
+            dma((nf * parts,)), dma((nt,)),
+            dma((4 * ny + 2 * nl,)), dma((4 * ny + 2 * nl,)),
+            dma((4 * ny,)), dma((4 * ny,)),
+            dma((4 * ny,)), dma((4 * ny,)),
+            dma((2 * nl,)), dma((2 * nl,)),
+            dma((2,)),
+        ],
+        compiler_params=pltpu.CompilerParams(
+            collective_id=0, has_side_effects=True, vmem_limit_bytes=VMEM_LIMIT
+        ),
+        cost_estimate=pl.CostEstimate(flops=flops, bytes_accessed=8 * nl * cols * width, transcendentals=0),
+    )(cap, target[0], enc_weight[0], enc_bias, dec_weight[0], dec_bias)
+    enc_grad, enc_bias_grad, dec_grads, dec_bias_grad = out
+    return (enc_grad[None], enc_bias_grad, dec_grads[None], dec_bias_grad)
+
+
+def fits(mesh):
+    return mesh.shape["feat"] == 2 and mesh.shape["tok"] % 2 == 0 and mesh.shape["tok"] >= 4
+
+
 def solution(mesh):
     in_specs = (
         P("layer", "tok", "feat"),
@@ -94,6 +479,7 @@
         P("layer", None, "feat", "tok"),
         P("layer", "tok"),
     )
+    body = functools.partial(on_device_fused, mesh) if fits(mesh) else on_device
     return jax.shard_map(
-        on_device, mesh=mesh, in_specs=in_specs, out_specs=out_specs, check_vma=False
-    )
+        body, mesh=mesh, in_specs=in_specs, out_specs=out_specs, check_vma=False
+    )

time: 364 us -> 137 us (0.38)
  waiting for transfers between devices: 263 us -> 0 us
  Pallas kernels: 0 us -> 116 us
  matrix products: 39.5 us -> 0 us
  blocking collectives: 28.5 us -> 0 us
  between operations: 14.2 us -> 0.66 us
  local copies, waits for them, and re-layouts: 9.27 us -> 20.1 us
  other arithmetic: 7.76 us -> 0 us
    reduce_scatter x4 -> x0, waiting for transfers between devices: 168 us -> none  [the longest x1 57.3 us: on_device(): lax.psum_scatter(partial_value, 'feat', scatter_dimension=1, tiled=True)]
    pallas_call x0 -> x1, Pallas kernels: none -> 116 us  [on_device_fused(): pl.pallas_call(functools.partial(fused_kernel, sizes), out_shape=(jax.Sha...]
    all_gather x4 -> x0, waiting for transfers between devices: 95 us -> none  [the longest x1 36.5 us: on_device(): grad_all = lax.all_gather(spread, 'feat', axis=1, tiled=True)]
    dot_general x14 -> x0, matrix products: 39.5 us -> none  [the longest x5 14.5 us: contract_rows(): lax.dot_general(left, right, (((0,), (0,)), ((), ())), preferred_element_...]
    unnamed x17 -> x11, local copies, waits for them, and re-layouts: 3.43 us -> 19.9 us
    all_to_all x1 -> x0, blocking collectives: 12.4 us -> none  [on_device(): moved = lax.all_to_all(rows, 'tok', split_axis=1, concat_axis=0, tiled=True)]
    all_gather x1 -> x0, blocking collectives: 10.6 us -> none  [on_device(): rows = lax.all_gather(captured[0], 'feat', axis=1, tiled=True)]
    broadcast_in_dim x3 -> x0, local copies, waits for them, and re-layouts: 5.82 us -> none  [the longest x1 2.79 us: on_device(): dec_start = jnp.zeros((nlayer, feat_cols, width_part), jnp.bfloat16)]
  transfers between devices with their start and end apart: 8 -> 0, of which waited for: 8 -> 0; matrix products, arithmetic and copies ran while one was open for 0% -> 0% of each run, Pallas kernels for 0% -> 0%
where the time goes in v1:
time: 137 us
  Pallas kernels  116 us (85%)
  local copies, waits for them, and re-layouts  20.1 us (15%)
    pallas_call x1, Pallas kernels, on_device_fused(): pl.pallas_call(functools.partial(fused_kernel, sizes), out_shape=(jax.Sha...  116 us
    unnamed x11, local copies, waits for them, and re-layouts  19.9 us

profile of v1, /device:TPU:0, one launch (start us, length us, event | category | flops | bytes accessed | tf_op | source)
XLA Modules:
  0.0 136.7 jit_solution(6397023683692562016)
XLA Ops:
  0.6 1.2 copy.13
  1.8 0.2 copy.14
  2.0 1.2 copy.15
  3.2 0.0 copy-start
  3.2 0.0 copy-start.1
  3.2 7.7 %copy.16 = bf16[1,4,1024,576]{3,2,1,0:T(8,128)(2,1)} copy(bf16[1,4,1024,576]{2,3,1,0:T(8,128)(2,1)} %param.10) | data formatting | bytes 9437184 | tf_op args[4]
  10.9 0.0 copy-done
  10.9 0.0 copy-done.1
  10.9 115.9 %shard_map.93 = (bf16[576,1024]{1,0:T(8,128)(2,1)S(1)}, f32[1,1024]{1,0:T(1,128)S(1)}, bf16[4,1024,576]{2,1,0:T(8,128)(2,1)}, f32[1,576]{1,0:T(1,128)S(1)}) custom-call(bf16[2,128,576]{2,1,0:T(8,128)(2,1)S(1)} %bitcast.8, bf16[256,576]{1,0:T(8,128)(2,1)S(1)} %bitcast.9, bf16[576,1024]{1,0:T(8,128)(2,1)} %bitcast.13, f32[1,1024]{1,0:T(1,128)S(1)} %copy-done, ...), custom_call_target="tpu_custom_call" | custom-call | flops 8455716864 | bytes 18874368 | tf_op jit(solution)/shard_map/pallas_call | solution.py:416
  126.9 7.6 %copy.17 = bf16[1,4,1024,576]{2,3,1,0:T(8,128)(2,1)} copy(bf16[1,4,1024,576]{3,2,1,0:T(8,128)(2,1)} %bitcast.10) | data formatting | bytes 9437184
  134.5 1.0 copy.21
  135.5 0.6 copy.22
  136.1 0.6 copy.23
Async XLA Ops:
  3.2 7.8 %copy-start = (f32[1,1024]{1,0:T(1,128)S(1)}, f32[1,1024]{1,0:T(1,128)}, u32[]{:S(2)}) copy-start(f32[1,1024]{1,0:T(1,128)} %enc_bias.1) | copy-start | bytes 12292
  3.2 7.8 %copy-start.1 = (f32[1,576]{1,0:T(1,128)S(1)}, f32[1,576]{1,0:T(1,128)}, u32[]{:S(2)}) copy-start(f32[1,576]{1,0:T(1,128)} %dec_bias.1) | copy-start | bytes 6916

commit v2 on v1

--- a/solution.py
+++ b/solution.py
@@ -89,10 +89,10 @@
 
 
 def fused_kernel(
-    sizes, cap, target, enc_hbm, enc_bias, dec_hbm, dec_bias,
+    sizes, cap_hbm, target_hbm, enc_hbm, enc_bias, dec_hbm, dec_bias,
     enc_grad, enc_bias_grad, dec_grad_hbm, dec_bias_grad,
-    enc, dec, blk, blk_t, pre_a, pre_b, pre_ra, pre_rb, pre_own, pre,
-    act, act_t, x_out, x_in, own, z_out, z_in, bias_out, bias_in, grad,
+    cap_in, cap, target, enc, dec, blk, blk_t, pre_a, pre_b, pre_ra, pre_rb, pre_own, pre,
+    act, x_out, x_in, own, z_out, z_in, bias_out, bias_in, grad,
     acc, back_a, back_b, back_ra, back_rb, grad_pre, dec_out,
     load_sem, store_sem, cap_send, cap_recv, pair_send, pair_recv,
     row_send, row_recv, fwd_send, fwd_recv, lay_send, lay_recv, bias_sem,
@@ -104,11 +104,15 @@
     sib = y * 2 + (1 - c)
     other = 1 - f
     parts, rows, width = cap.shape
-    half = target.shape[0]
+    half = target.shape[1]
 
     load_enc = pltpu.make_async_copy(enc_hbm, enc, load_sem.at[0])
     load_dec = pltpu.make_async_copy(dec_hbm, dec, load_sem.at[1])
+    load_target = pltpu.make_async_copy(target_hbm, target, load_sem.at[2])
+    load_cap = pltpu.make_async_copy(cap_hbm, cap_in, load_sem.at[3])
+    load_cap.start()
     load_enc.start()
+    load_target.start()
     load_dec.start()
 
     barrier = pltpu.get_barrier_semaphore()
@@ -127,6 +131,9 @@
         pl.semaphore_signal(barrier, inc=1, device_id={"layer": l + 1}, device_id_type=MESH)
 
     layer_peers = jnp.where(l > 0, 1, 0) + jnp.where(l < nl - 1, 1, 0)
+    load_cap.wait()
+    for p in range(parts):
+        cap[p] = cap_in[:, p * width:(p + 1) * width]
     pl.semaphore_wait(barrier, nf * nt - 1 + layer_peers)
 
     def remote(source, dest, send, recv, **where):
@@ -262,17 +269,21 @@
             z_out.at[write], z_in.at[write], lay_send.at[write], lay_recv.at[write], feat=other
         ).wait_recv()
 
+    def decoded(write, which):
+        return lax.dot_general(
+            dec[write], act[half_rows(which), :], (((1,), (1,)), ((), ())),
+            preferred_element_type=F32,
+        )
+
     def decode_other(i, carry):
         write = nl - 1 - i
-        x_out[write] = jnp.dot(
-            act[half_rows(other), :], dec[write], preferred_element_type=F32
-        ).astype(BF16)
+        x_out[write] = decoded(write, other).astype(BF16)
         x_copy(write).start()
         return carry
 
     def decode_own(i, carry):
         write = nl - 1 - i
-        own[write] = jnp.dot(act[half_rows(f), :], dec[write], preferred_element_type=F32)
+        own[write] = decoded(write, f)
         return carry
 
     def decode_sum(i, carry):
@@ -293,34 +304,34 @@
 
     lax.fori_loop(0, nl - l, decode_other, 0)
     lax.fori_loop(0, nl - l, decode_own, 0)
-    for b in range(nt):
-        act_t[:, b * rows:(b + 1) * rows] = act[b * rows:(b + 1) * rows, :].T
+    load_target.wait()
+    bias_col = jnp.broadcast_to(dec_bias[...], (8, width)).T[:, 0:1]
     lax.fori_loop(0, nl - l, decode_sum, 0)
 
-    scaled = (own[l] + dec_bias[...] - target[...].astype(F32)) * scale
-    grad[l, half_rows(f), :] = scaled.astype(BF16)
+    scaled = (own[l] + bias_col - target[...].astype(F32)) * scale
+    grad[l, :, half_rows(f)] = scaled.astype(BF16)
 
     def down_copy(write):
-        tile = grad.at[write, half_rows(f)]
+        tile = grad.at[write, :, half_rows(f)]
         return remote(
             tile, tile, lay_send.at[nl + write], lay_recv.at[nl + write], layer=l - 1
         )
 
     def down_wait(write):
-        tile = grad.at[write, half_rows(f)]
+        tile = grad.at[write, :, half_rows(f)]
         remote(
             tile, tile, lay_send.at[nl + write], lay_recv.at[nl + write], feat=other
         ).wait_recv()
 
     def across_copy(write):
-        tile = grad.at[write, half_rows(f)]
+        tile = grad.at[write, :, half_rows(f)]
         return remote(
             tile, tile, pair_send.at[4 * ny + nl + write], pair_recv.at[4 * ny + nl + write],
             feat=other,
         )
 
     def across_wait(write):
-        tile = grad.at[write, half_rows(other)]
+        tile = grad.at[write, :, half_rows(other)]
         remote(
             tile, tile, pair_send.at[4 * ny + nl + write], pair_recv.at[4 * ny + nl + write],
             feat=other,
@@ -333,12 +344,12 @@
         across_copy(write).start()
 
     pass_on(l)
-    bias_out[...] = jnp.broadcast_to(jnp.sum(scaled, axis=0, keepdims=True), bias_out.shape)
+    bias_out[...] = jnp.broadcast_to(jnp.sum(scaled, axis=1, keepdims=True), (width, 128)).T[0:8, :]
     bias_copy = remote(bias_out, bias_in, bias_sem.at[0], bias_sem.at[1], feat=other)
     bias_copy.start()
 
     def dec_grad_of(write):
-        dec_out[write] = jnp.dot(act_t[...], grad[write], preferred_element_type=F32).astype(BF16)
+        dec_out[write] = jnp.dot(grad[write], act[...], preferred_element_type=F32).astype(BF16)
         pltpu.make_async_copy(dec_out.at[write], dec_grad_hbm.at[write], store_sem.at[write]).start()
 
     def back_step(write, carry):
@@ -348,7 +359,7 @@
             pass_on(write + 1)
         across_wait(write)
         acc[...] += lax.dot_general(
-            grad[write], dec[write], (((1,), (1,)), ((), ())), preferred_element_type=F32
+            grad[write], dec[write], (((0,), (0,)), ((), ())), preferred_element_type=F32
         )
 
         @pl.when(write < nl - 1)
@@ -404,46 +415,47 @@
     half = target.shape[1]
     tokens = rows * nt
     parts = captured.shape[2] // width
-    cap = captured[0].reshape(rows, parts, width).transpose(1, 0, 2)
     sizes = (nf, nl, nt, 1.0 / math.sqrt(tokens))
     vm = pl.BlockSpec(memory_space=pltpu.VMEM)
     hbm = pl.BlockSpec(memory_space=pl.ANY)
     dma = pltpu.SemaphoreType.DMA
     block32 = pltpu.VMEM((ny, rows, cols), F32)
     block16 = pltpu.VMEM((ny, rows, cols), BF16)
-    tile16 = pltpu.VMEM((nl, half, width), BF16)
+    tile16 = pltpu.VMEM((nl, width, half), BF16)
     flops = 2 * tokens * width * cols * (2 + 3 * nl)
     out = pl.pallas_call(
         functools.partial(fused_kernel, sizes),
         out_shape=(
             jax.ShapeDtypeStruct((width, cols), BF16),
             jax.ShapeDtypeStruct((1, cols), F32),
-            jax.ShapeDtypeStruct((nl, cols, width), BF16),
+            jax.ShapeDtypeStruct((nl, width, cols), BF16),
             jax.ShapeDtypeStruct((1, width), F32),
         ),
-        in_specs=[vm, vm, hbm, vm, hbm, vm],
+        in_specs=[hbm, hbm, hbm, vm, hbm, vm],
         out_specs=(vm, vm, hbm, vm),
         scratch_shapes=[
+            pltpu.VMEM((rows, parts * width), BF16),
+            pltpu.VMEM((parts, rows, width), BF16),
+            pltpu.VMEM((width, half), BF16),
             pltpu.VMEM((width, cols), BF16),
-            pltpu.VMEM((nl, cols, width), BF16),
+            pltpu.VMEM((nl, width, cols), BF16),
             pltpu.VMEM((tokens, width), BF16),
             pltpu.VMEM((width, tokens), BF16),
             block32, block32, block32, block32,
             pltpu.VMEM((rows, cols), F32),
             pltpu.VMEM((rows, cols), F32),
             pltpu.VMEM((tokens, cols), BF16),
-            pltpu.VMEM((cols, tokens), BF16),
             tile16, tile16,
-            pltpu.VMEM((nl, half, width), F32),
+            pltpu.VMEM((nl, width, half), F32),
             tile16, tile16,
             pltpu.VMEM((8, width), F32),
             pltpu.VMEM((8, width), F32),
-            pltpu.VMEM((nl, tokens, width), BF16),
+            pltpu.VMEM((nl, width, tokens), BF16),
             pltpu.VMEM((tokens, cols), F32),
             block16, block16, block16, block16,
             pltpu.VMEM((tokens, cols), BF16),
-            pltpu.VMEM((nl, cols, width), BF16),
-            dma((2,)), dma((nl,)),
+            pltpu.VMEM((nl, width, cols), BF16),
+            dma((4,)), dma((nl,)),
             dma((nf * parts,)), dma((nt,)),
             dma((4 * ny + 2 * nl,)), dma((4 * ny + 2 * nl,)),
             dma((4 * ny,)), dma((4 * ny,)),
@@ -455,9 +467,9 @@
             collective_id=0, has_side_effects=True, vmem_limit_bytes=VMEM_LIMIT
         ),
         cost_estimate=pl.CostEstimate(flops=flops, bytes_accessed=8 * nl * cols * width, transcendentals=0),
-    )(cap, target[0], enc_weight[0], enc_bias, dec_weight[0], dec_bias)
+    )(captured[0], target[0].T, enc_weight[0], enc_bias, dec_weight[0].swapaxes(1, 2), dec_bias)
     enc_grad, enc_bias_grad, dec_grads, dec_bias_grad = out
-    return (enc_grad[None], enc_bias_grad, dec_grads[None], dec_bias_grad)
+    return (enc_grad[None], enc_bias_grad, dec_grads.swapaxes(1, 2)[None], dec_bias_grad)
 
 
 def fits(mesh):

time: 137 us -> 123 us (0.90)
  local copies, waits for them, and re-layouts: 20.1 us -> 10.5 us
  Pallas kernels: 116 us -> 111 us
    unnamed x11 -> x12, local copies, waits for them, and re-layouts: 19.9 us -> 10.5 us
    pallas_call x1, Pallas kernels: 116 us -> 111 us  [on_device_fused(): pl.pallas_call(functools.partial(fused_kernel, sizes), out_shape=(jax.Sha...]
where the time goes in v2:
time: 123 us
  Pallas kernels  111 us (90%)
  local copies, waits for them, and re-layouts  10.5 us (9%)
    pallas_call x1, Pallas kernels, on_device_fused(): pl.pallas_call(functools.partial(fused_kernel, sizes), out_shape=(jax.Sha...  111 us
    unnamed x12, local copies, waits for them, and re-layouts  10.5 us

profile of v2, /device:TPU:0, one launch (start us, length us, event | category | flops | bytes accessed | tf_op | source)
XLA Modules:
  0.0 122.6 jit_solution(11584395488052194983)
XLA Ops:
  0.6 0.0 copy-start
  0.6 1.0 copy-done
  1.6 0.0 copy-start.1
  1.6 1.0 copy-done.1
  2.6 0.0 copy-start.2
  2.6 0.7 copy-done.2
  3.2 0.0 copy-start.3
  3.2 0.7 copy-done.3
  3.9 111.5 %shard_map.93 = (bf16[576,1024]{1,0:T(8,128)(2,1)S(1)}, f32[1,1024]{1,0:T(1,128)S(1)}, bf16[4,576,1024]{2,1,0:T(8,128)(2,1)}, f32[1,576]{1,0:T(1,128)S(1)}) custom-call(bf16[128,1152]{1,0:T(8,128)(2,1)S(1)} %bitcast.13, bf16[576,256]{1,0:T(8,128)(2,1)S(1)} %bitcast.14, bf16[576,1024]{1,0:T(8,128)(2,1)} %bitcast.17, f32[1,1024]{1,0:T(1,128)S(1)} %copy-done.2, ...), custom_call_target="tpu_custom_call" | custom-call | flops 8455716864 | bytes 18874368 | tf_op jit(solution)/shard_map/pallas_call | solution.py:426
  115.4 1.0 copy.14
  116.4 0.6 copy.15
  117.0 5.0 %copy.16 = bf16[1,4,1024,576]{2,3,1,0:T(8,128)(2,1)} copy(bf16[1,4,1024,576]{2,3,1,0:T(8,128)(2,1)} %bitcast.15) | data formatting | bytes 9437184
  122.1 0.6 copy.17
Async XLA Ops:
  0.6 1.0 copy-start
  1.6 1.0 copy-start.1
  2.6 0.7 copy-start.2
  3.2 0.7 copy-start.3

commit v3 on v2

--- a/solution.py
+++ b/solution.py
@@ -85,13 +85,13 @@
 BF16 = jnp.bfloat16
 F32 = jnp.float32
 MESH = pl.DeviceIdType.MESH
-VMEM_LIMIT = 52 * 1024 * 1024
+VMEM_LIMIT = 60 * 1024 * 1024
 
 
 def fused_kernel(
-    sizes, cap_hbm, target_hbm, enc_hbm, enc_bias, dec_hbm, dec_bias,
+    sizes, cap_hbm, target_hbm, enc_hbm, enc_bias_hbm, dec_hbm, dec_bias_hbm,
     enc_grad, enc_bias_grad, dec_grad_hbm, dec_bias_grad,
-    cap_in, cap, target, enc, dec, blk, blk_t, pre_a, pre_b, pre_ra, pre_rb, pre_own, pre,
+    enc_bias, dec_bias, cap_in, cap, target, enc, dec, blk, blk_t, pre_a, pre_b, pre_ra, pre_rb, pre_own, pre,
     act, x_out, x_in, own, z_out, z_in, bias_out, bias_in, grad,
     acc, back_a, back_b, back_ra, back_rb, grad_pre, dec_out,
     load_sem, store_sem, cap_send, cap_recv, pair_send, pair_recv,
@@ -110,10 +110,14 @@
     load_dec = pltpu.make_async_copy(dec_hbm, dec, load_sem.at[1])
     load_target = pltpu.make_async_copy(target_hbm, target, load_sem.at[2])
     load_cap = pltpu.make_async_copy(cap_hbm, cap_in, load_sem.at[3])
+    load_enc_bias = pltpu.make_async_copy(enc_bias_hbm, enc_bias, load_sem.at[4])
+    load_dec_bias = pltpu.make_async_copy(dec_bias_hbm, dec_bias, load_sem.at[5])
     load_cap.start()
     load_enc.start()
     load_target.start()
     load_dec.start()
+    load_enc_bias.start()
+    load_dec_bias.start()
 
     barrier = pltpu.get_barrier_semaphore()
     for df in range(nf):
@@ -186,8 +190,7 @@
             ).wait_recv()
         return jnp.dot(blk[token_rows(block), :], enc[...], preferred_element_type=F32)
 
-    def reduce_rows(base, partial, out_a, out_b, in_a, in_b, kept):
-        order = list(range(1, ny)) + [0]
+    def reduce_rows(base, order, partial, out_a, out_b, in_a, in_b, kept):
         firsts, seconds = {}, {}
         for dy in order:
             yb = (y + dy) % ny
@@ -245,9 +248,10 @@
         for copy in [direct] + across + forwards:
             copy.wait_send()
 
-    finish = reduce_rows(0, encode, pre_a, pre_b, pre_ra, pre_rb, pre_own)
+    finish = reduce_rows(0, list(range(ny)), encode, pre_a, pre_b, pre_ra, pre_rb, pre_own)
     for b in range(nt):
         blk_t[:, b * rows:(b + 1) * rows] = blk[b * rows:(b + 1) * rows, :].T
+    load_enc_bias.wait()
     pre[...] = finish() + enc_bias[...]
     act[token_rows(t), :] = jnp.maximum(pre[...], 0.0).astype(BF16)
     gather_rows(ny, act)
@@ -305,6 +309,7 @@
     lax.fori_loop(0, nl - l, decode_other, 0)
     lax.fori_loop(0, nl - l, decode_own, 0)
     load_target.wait()
+    load_dec_bias.wait()
     bias_col = jnp.broadcast_to(dec_bias[...], (8, width)).T[:, 0:1]
     lax.fori_loop(0, nl - l, decode_sum, 0)
 
@@ -370,7 +375,8 @@
     lax.fori_loop(l, nl, back_step, 0)
 
     finish = reduce_rows(
-        2 * ny, lambda block: acc[token_rows(block), :], back_a, back_b, back_ra, back_rb, pre_own
+        2 * ny, list(range(1, ny)) + [0], lambda block: acc[token_rows(block), :],
+        back_a, back_b, back_ra, back_rb, pre_own,
     )
     dec_grad_of(nl - 1)
     grad_pre[token_rows(t), :] = jnp.where(pre[...] > 0, finish(), 0.0).astype(BF16)
@@ -405,6 +411,24 @@
     lax.fori_loop(l, nl, drain, 0)
     for write in range(nl):
         pltpu.make_async_copy(dec_out.at[write], dec_grad_hbm.at[write], store_sem.at[write]).wait()
+
+
+def store_kernel(count, *refs):
+    sources, dests, held = (refs[i * count:(i + 1) * count] for i in range(3))
+    load_sem, store_sem = refs[3 * count:]
+    loads, stores = [], []
+    for source, dest, block in zip(sources, dests, held):
+        for part in range(source.shape[0]):
+            n = len(loads)
+            loads.append(pltpu.make_async_copy(source.at[part], block.at[part], load_sem.at[n]))
+            stores.append(pltpu.make_async_copy(block.at[part], dest.at[part], store_sem.at[n]))
+    for load in loads:
+        load.start()
+    for load, store in zip(loads, stores):
+        load.wait()
+        store.start()
+    for store in stores:
+        store.wait()
 
 
 def on_device_fused(mesh, captured, target, enc_weight, enc_bias, dec_weight, dec_bias):
@@ -431,9 +455,11 @@
             jax.ShapeDtypeStruct((nl, width, cols), BF16),
             jax.ShapeDtypeStruct((1, width), F32),
         ),
-        in_specs=[hbm, hbm, hbm, vm, hbm, vm],
+        in_specs=[pl.BlockSpec(memory_space=pltpu.HBM)] * 6,
         out_specs=(vm, vm, hbm, vm),
         scratch_shapes=[
+            pltpu.VMEM((1, cols), F32),
+            pltpu.VMEM((1, width), F32),
             pltpu.VMEM((rows, parts * width), BF16),
             pltpu.VMEM((parts, rows, width), BF16),
             pltpu.VMEM((width, half), BF16),
@@ -455,7 +481,7 @@
             block16, block16, block16, block16,
             pltpu.VMEM((tokens, cols), BF16),
             pltpu.VMEM((nl, width, cols), BF16),
-            dma((4,)), dma((nl,)),
+            dma((6,)), dma((nl,)),
             dma((nf * parts,)), dma((nt,)),
             dma((4 * ny + 2 * nl,)), dma((4 * ny + 2 * nl,)),
             dma((4 * ny,)), dma((4 * ny,)),
@@ -469,7 +495,17 @@
         cost_estimate=pl.CostEstimate(flops=flops, bytes_accessed=8 * nl * cols * width, transcendentals=0),
     )(captured[0], target[0].T, enc_weight[0], enc_bias, dec_weight[0].swapaxes(1, 2), dec_bias)
     enc_grad, enc_bias_grad, dec_grads, dec_bias_grad = out
-    return (enc_grad[None], enc_bias_grad, dec_grads.swapaxes(1, 2)[None], dec_bias_grad)
+    out = (enc_grad[None], enc_bias_grad[None], dec_grads, dec_bias_grad[None])
+    enc_grad, enc_bias_grad, dec_grads, dec_bias_grad = pl.pallas_call(
+        functools.partial(store_kernel, len(out)),
+        out_shape=[jax.ShapeDtypeStruct(part.shape, part.dtype) for part in out],
+        in_specs=[hbm] * len(out),
+        out_specs=[hbm] * len(out),
+        scratch_shapes=[pltpu.VMEM(part.shape, part.dtype) for part in out]
+        + [dma((sum(part.shape[0] for part in out),))] * 2,
+        compiler_params=pltpu.CompilerParams(vmem_limit_bytes=VMEM_LIMIT),
+    )(*out)
+    return (enc_grad, enc_bias_grad[0], dec_grads.swapaxes(1, 2)[None], dec_bias_grad[0])
 
 
 def fits(mesh):

time: 123 us -> 118 us (0.959)
  local copies, waits for them, and re-layouts: 10.5 us -> 0 us
  Pallas kernels: 111 us -> 117 us
    unnamed x12 -> x0, local copies, waits for them, and re-layouts: 10.5 us -> none
    pallas_call x0 -> x1, Pallas kernels: none -> 5.05 us  [on_device_fused(): pl.pallas_call(functools.partial(store_kernel, len(out)), out_shape=[jax....]
where the time goes in v3:
time: 118 us
  Pallas kernels  117 us (99%)
    pallas_call x1, Pallas kernels, on_device_fused(): pl.pallas_call(functools.partial(fused_kernel, sizes), out_shape=(jax.Sha...  112 us
    pallas_call x1, Pallas kernels, on_device_fused(): pl.pallas_call(functools.partial(store_kernel, len(out)), out_shape=[jax....  5.05 us

profile of v3, /device:TPU:0, one launch (start us, length us, event | category | flops | bytes accessed | tf_op | source)
XLA Modules:
  0.0 118.0 jit_solution(2836520618273969892)
XLA Ops:
  0.6 112.3 %shard_map.93 = (bf16[576,1024]{1,0:T(8,128)(2,1)}, f32[1,1024]{1,0:T(1,128)}, bf16[4,576,1024]{2,1,0:T(8,128)(2,1)}, f32[1,576]{1,0:T(1,128)}) custom-call(bf16[128,1152]{1,0:T(8,128)(2,1)} %bitcast.22, bf16[576,256]{1,0:T(8,128)(2,1)} %bitcast.23, bf16[576,1024]{1,0:T(8,128)(2,1)} %bitcast.21, f32[1,1024]{1,0:T(1,128)} %enc_bias_hbm.1, ...), custom_call_target="tpu_custom_call" | custom-call | flops 8455716864 | bytes 18874368 | tf_op jit(solution)/shard_map/pallas_call | solution.py:450
  112.9 5.0 %shard_map.94 = (bf16[1,576,1024]{2,1,0:T(8,128)(2,1)}, f32[1,1,1024]{2,1,0:T(1,128)}, bf16[4,576,1024]{2,1,0:T(8,128)(2,1)}, f32[1,1,576]{2,1,0:T(1,128)}) custom-call(bf16[1,576,1024]{2,1,0:T(8,128)(2,1)} %bitcast.16, f32[1,1,1024]{2,1,0:T(1,128)} %bitcast.17, bf16[4,576,1024]{2,1,0:T(8,128)(2,1)} %get-tuple-element.14.refs_2_, f32[1,1,576]{2,1,0:T(1,128)} %bitcast.18), custom_call_target="tpu_custom_call" | custom-call | tf_op jit(solution)/shard_map/pallas_call | solution.py:499
